TPU v7x, 32 devices: a whole 2x2x4 slice. The times are simulated.
32 devices in a mesh: vp: 8 (over z, x), vc: 4 (over y, core).
Axes of the slice: x: 2, y: 2, z: 4, core: 2. Of those that a mesh axis runs over, the one named last changes fastest.
Arguments:
- amplitudes: bfloat16 [64, 102400], P(('vp', 'vc')), may hold values from -6 to 6
- pair_tiles: bfloat16 [8192, 128, 128], P(('vp', 'vc')), may hold values from -0.09375 to 0.09375
- slot_pairs: int32 [8192, 2], P(('vp', 'vc')), may hold values from 0 to 199, as said below
- slot_count: int32 [32], P(('vp', 'vc')), may hold values from 32 to 256, as said below
Outputs:
- ladder: bfloat16 [64, 16384], P('vc', 'vp')
Inputs may be any that keep to these rules, and one draw needn't show every extreme that they name: `slot_pairs`: the rows of one device name distinct pairs; column 0 lies in 0 to 15, column 1 in 0 to 199. `slot_count`: every count is 256 divided by 1, 2, 4 or 8; some device has exactly 256.
All inputs are finite; a program needn't handle non-finite values.
Results may differ from a plain program's by a relative error of at most 0.001.
Values may be sent and summed in bfloat16 or wider, within the bound.
A program may use at most 128 MiB of HBM per device.

v0:
```python
import math

import jax
import jax.numpy as jnp
from jax import lax
from jax.sharding import PartitionSpec as P

ABT_DEV = 16


def accumulate(amp_rows, tiles_all, table_all, end_slot, ab_tiles):
    row_total = amp_rows.shape[0]
    tile_width = tiles_all.shape[1]
    grouped = amp_rows.reshape(row_total, -1, tile_width)
    block_size = math.gcd(32, tiles_all.shape[0])
    end_block = (end_slot + block_size - 1) // block_size

    def add_block(block_index, totals):
        offset = block_index * block_size
        tiles_block = lax.dynamic_slice_in_dim(tiles_all, offset, block_size, 0)
        indices = lax.dynamic_slice_in_dim(table_all, offset, block_size, 0)
        slot_ids = offset + jnp.arange(block_size, dtype=jnp.int32)
        alive_mask = (slot_ids < end_slot).astype(jnp.float32)
        picked = jnp.take(grouped, indices[:, 1], axis=1)
        product = jnp.einsum(
            "pkc,kcn->pkn", picked, tiles_block, preferred_element_type=jnp.float32
        )
        select = (indices[:, 0][:, None] == jnp.arange(ab_tiles, dtype=jnp.int32)[None, :]).astype(
            jnp.float32
        ) * alive_mask[:, None]
        return totals + jnp.einsum("pkn,ka->pan", product, select, precision=lax.Precision.HIGHEST)

    start_totals = jnp.zeros((row_total, ab_tiles, tile_width), jnp.float32)
    totals = lax.fori_loop(0, end_block, add_block, start_totals)
    return totals.reshape(row_total, ab_tiles * tile_width)


def per_device(amplitudes, pair_tiles, slot_pairs, slot_count):
    ab_tiles = ABT_DEV
    columns = lax.all_to_all(amplitudes, "vc", split_axis=1, concat_axis=0, tiled=True)
    partial_value = accumulate(
        lax.all_gather(columns, "vp", axis=0, tiled=True),
        pair_tiles,
        slot_pairs,
        slot_count[0],
        ab_tiles,
    )
    result = lax.psum_scatter(partial_value, "vc", scatter_dimension=0, tiled=True)
    return result.astype(jnp.bfloat16)


def solution(mesh):
    in_specs = (
        P(("vp", "vc"), None),
        P(("vp", "vc"), None, None),
        P(("vp", "vc"), None),
        P(("vp", "vc")),
    )
    out_specs = P("vc", "vp")
    return jax.shard_map(
        per_device, mesh=mesh, in_specs=in_specs, out_specs=out_specs, check_vma=False
    )
```

profile of v0, /device:TPU:1, one launch (start us, length us, event | category | flops | bytes accessed | tf_op | source)
XLA Modules:
  0.0 167.3 jit_solution(17766226427044461378)
XLA Ops:
  6.5 11.4 %all_to_all.19 = bf16[2,4,25600]{2,0,1:T(2,128)(2,1)S(1)} all-to-all(bf16[2,4,25600]{2,0,1:T(2,128)(2,1)} %bitcast.46), channel_id=1, replica_groups=mesh['vp'=8,'vc'=4] {'vc'}, dimensions={1} | all-to-all | bytes 819200 | tf_op jit(solution)/shard_map/all_to_all | solution.py:40
  19.6 61.3 %all-gather.2.cloned.1.call-done = bf16[64,25600]{1,0:T(8,128)(2,1)} async-done(((bf16[8,25600]{1,0:T(8,128)(2,1)}), bf16[64,25600]{1,0:T(8,128)(2,1)}) %all-gather.2.cloned.1.call-update) | async-done | bytes 3276816 | tf_op jit(solution)/shard_map/all_gather | solution.py:42
  80.9 4.5 %copy_bitcast_fusion = bf16[64,200,128]{2,0,1:T(8,128)(2,1)} fusion(bf16[64,25600]{1,0:T(8,128)(2,1)} %all-gather.2.cloned.1.call-done), kind=kLoop, calls=%fused_computation.26 | loop fusion | bytes 6553600 | tf_op jit(solution)/shard_map/while | solution.py:34
  85.5 51.2 %while.10 = (s32[]{:T(128)}, f32[64,16,128]{2,1,0:T(8,128)S(1)}, s32[]{:T(128)}, s32[256,2]{0,1:T(2,128)S(1)}, s32[]{:T(128)}, /*index=5*/bf16[256,128,128]{2,1,...) while((s32[]{:T(128)}, f32[64,16,128]{2,1,0:T(8,128)S(1)}, ...), condition=%wide.region_1.2_spmd, body=%wide.region_0.1_spmd.sunk | while | flops 117836168 | bytes 5773291 | solution.py:34
  85.6 2.6 %gather_fusion = bf16[32,64,128]{2,1,0:T(8,128)(2,1)S(1)} fusion(bf16[64,200,128]{2,0,1:T(8,128)(2,1)} %get-tuple-element.143, s32[1024]{0:T(1024)S(1)} %pad_clamp_fusion.2), kind=kCustom, calls=%fused_computation.clone.1 | custom fusion | bytes 1048704 | tf_op jit(solution)/shard_map/while/body/jit(_take)/gather | solution.py:24
  88.2 1.7 %convolution_bitcast_fusion.3 = f32[64,32,128]{2,0,1:T(8,128)S(1)} fusion(bf16[256,128,128]{2,1,0:T(8,128)(2,1)} %get-tuple-element.142, s32[]{:T(128)S(6)} %select_n.36, bf16[32,64,128]{2,1,0:T(8,128)(2,1)S(1)} %gather_fusion, pred[32]{0:T(512)(128)(4,1)S(1)} %and_bitcast_fusion.2), kind=kOutput, calls=%fused_computation.1.clone.1 | convolution fusion | flops 67371008 | bytes 2621476 | tf_op jit(solution)/shard_map/while/body/pkc,kcn->pkn/dot_general | solution.py:25
  90.5 1.3 fusion.26
  92.0 2.6 %gather_fusion = bf16[32,64,128]{2,1,0:T(8,128)(2,1)S(1)} fusion(bf16[64,200,128]{2,0,1:T(8,128)(2,1)} %get-tuple-element.143, s32[1024]{0:T(1024)S(1)} %pad_clamp_fusion.2), kind=kCustom, calls=%fused_computation.clone.1 | custom fusion | bytes 1048704 | tf_op jit(solution)/shard_map/while/body/jit(_take)/gather | solution.py:24
  94.6 1.7 %convolution_bitcast_fusion.3 = f32[64,32,128]{2,0,1:T(8,128)S(1)} fusion(bf16[256,128,128]{2,1,0:T(8,128)(2,1)} %get-tuple-element.142, s32[]{:T(128)S(6)} %select_n.36, bf16[32,64,128]{2,1,0:T(8,128)(2,1)S(1)} %gather_fusion, pred[32]{0:T(512)(128)(4,1)S(1)} %and_bitcast_fusion.2), kind=kOutput, calls=%fused_computation.1.clone.1 | convolution fusion | flops 67371008 | bytes 2621476 | tf_op jit(solution)/shard_map/while/body/pkc,kcn->pkn/dot_general | solution.py:25
  96.9 1.3 fusion.26
  98.4 2.6 %gather_fusion = bf16[32,64,128]{2,1,0:T(8,128)(2,1)S(1)} fusion(bf16[64,200,128]{2,0,1:T(8,128)(2,1)} %get-tuple-element.143, s32[1024]{0:T(1024)S(1)} %pad_clamp_fusion.2), kind=kCustom, calls=%fused_computation.clone.1 | custom fusion | bytes 1048704 | tf_op jit(solution)/shard_map/while/body/jit(_take)/gather | solution.py:24
  101.0 1.7 %convolution_bitcast_fusion.3 = f32[64,32,128]{2,0,1:T(8,128)S(1)} fusion(bf16[256,128,128]{2,1,0:T(8,128)(2,1)} %get-tuple-element.142, s32[]{:T(128)S(6)} %select_n.36, bf16[32,64,128]{2,1,0:T(8,128)(2,1)S(1)} %gather_fusion, pred[32]{0:T(512)(128)(4,1)S(1)} %and_bitcast_fusion.2), kind=kOutput, calls=%fused_computation.1.clone.1 | convolution fusion | flops 67371008 | bytes 2621476 | tf_op jit(solution)/shard_map/while/body/pkc,kcn->pkn/dot_general | solution.py:25
  104.8 2.6 %gather_fusion = bf16[32,64,128]{2,1,0:T(8,128)(2,1)S(1)} fusion(bf16[64,200,128]{2,0,1:T(8,128)(2,1)} %get-tuple-element.143, s32[1024]{0:T(1024)S(1)} %pad_clamp_fusion.2), kind=kCustom, calls=%fused_computation.clone.1 | custom fusion | bytes 1048704 | tf_op jit(solution)/shard_map/while/body/jit(_take)/gather | solution.py:24
  107.4 1.7 %convolution_bitcast_fusion.3 = f32[64,32,128]{2,0,1:T(8,128)S(1)} fusion(bf16[256,128,128]{2,1,0:T(8,128)(2,1)} %get-tuple-element.142, s32[]{:T(128)S(6)} %select_n.36, bf16[32,64,128]{2,1,0:T(8,128)(2,1)S(1)} %gather_fusion, pred[32]{0:T(512)(128)(4,1)S(1)} %and_bitcast_fusion.2), kind=kOutput, calls=%fused_computation.1.clone.1 | convolution fusion | flops 67371008 | bytes 2621476 | tf_op jit(solution)/shard_map/while/body/pkc,kcn->pkn/dot_general | solution.py:25
  111.2 2.6 %gather_fusion = bf16[32,64,128]{2,1,0:T(8,128)(2,1)S(1)} fusion(bf16[64,200,128]{2,0,1:T(8,128)(2,1)} %get-tuple-element.143, s32[1024]{0:T(1024)S(1)} %pad_clamp_fusion.2), kind=kCustom, calls=%fused_computation.clone.1 | custom fusion | bytes 1048704 | tf_op jit(solution)/shard_map/while/body/jit(_take)/gather | solution.py:24
  113.8 1.7 %convolution_bitcast_fusion.3 = f32[64,32,128]{2,0,1:T(8,128)S(1)} fusion(bf16[256,128,128]{2,1,0:T(8,128)(2,1)} %get-tuple-element.142, s32[]{:T(128)S(6)} %select_n.36, bf16[32,64,128]{2,1,0:T(8,128)(2,1)S(1)} %gather_fusion, pred[32]{0:T(512)(128)(4,1)S(1)} %and_bitcast_fusion.2), kind=kOutput, calls=%fused_computation.1.clone.1 | convolution fusion | flops 67371008 | bytes 2621476 | tf_op jit(solution)/shard_map/while/body/pkc,kcn->pkn/dot_general | solution.py:25
  117.6 2.6 %gather_fusion = bf16[32,64,128]{2,1,0:T(8,128)(2,1)S(1)} fusion(bf16[64,200,128]{2,0,1:T(8,128)(2,1)} %get-tuple-element.143, s32[1024]{0:T(1024)S(1)} %pad_clamp_fusion.2), kind=kCustom, calls=%fused_computation.clone.1 | custom fusion | bytes 1048704 | tf_op jit(solution)/shard_map/while/body/jit(_take)/gather | solution.py:24
  120.2 1.7 %convolution_bitcast_fusion.3 = f32[64,32,128]{2,0,1:T(8,128)S(1)} fusion(bf16[256,128,128]{2,1,0:T(8,128)(2,1)} %get-tuple-element.142, s32[]{:T(128)S(6)} %select_n.36, bf16[32,64,128]{2,1,0:T(8,128)(2,1)S(1)} %gather_fusion, pred[32]{0:T(512)(128)(4,1)S(1)} %and_bitcast_fusion.2), kind=kOutput, calls=%fused_computation.1.clone.1 | convolution fusion | flops 67371008 | bytes 2621476 | tf_op jit(solution)/shard_map/while/body/pkc,kcn->pkn/dot_general | solution.py:25
  124.0 2.6 %gather_fusion = bf16[32,64,128]{2,1,0:T(8,128)(2,1)S(1)} fusion(bf16[64,200,128]{2,0,1:T(8,128)(2,1)} %get-tuple-element.143, s32[1024]{0:T(1024)S(1)} %pad_clamp_fusion.2), kind=kCustom, calls=%fused_computation.clone.1 | custom fusion | bytes 1048704 | tf_op jit(solution)/shard_map/while/body/jit(_take)/gather | solution.py:24
  126.6 1.7 %convolution_bitcast_fusion.3 = f32[64,32,128]{2,0,1:T(8,128)S(1)} fusion(bf16[256,128,128]{2,1,0:T(8,128)(2,1)} %get-tuple-element.142, s32[]{:T(128)S(6)} %select_n.36, bf16[32,64,128]{2,1,0:T(8,128)(2,1)S(1)} %gather_fusion, pred[32]{0:T(512)(128)(4,1)S(1)} %and_bitcast_fusion.2), kind=kOutput, calls=%fused_computation.1.clone.1 | convolution fusion | flops 67371008 | bytes 2621476 | tf_op jit(solution)/shard_map/while/body/pkc,kcn->pkn/dot_general | solution.py:25
  130.4 2.6 %gather_fusion = bf16[32,64,128]{2,1,0:T(8,128)(2,1)S(1)} fusion(bf16[64,200,128]{2,0,1:T(8,128)(2,1)} %get-tuple-element.143, s32[1024]{0:T(1024)S(1)} %pad_clamp_fusion.2), kind=kCustom, calls=%fused_computation.clone.1 | custom fusion | bytes 1048704 | tf_op jit(solution)/shard_map/while/body/jit(_take)/gather | solution.py:24
  133.0 1.7 %convolution_bitcast_fusion.3 = f32[64,32,128]{2,0,1:T(8,128)S(1)} fusion(bf16[256,128,128]{2,1,0:T(8,128)(2,1)} %get-tuple-element.142, s32[]{:T(128)S(6)} %select_n.36, bf16[32,64,128]{2,1,0:T(8,128)(2,1)S(1)} %gather_fusion, pred[32]{0:T(512)(128)(4,1)S(1)} %and_bitcast_fusion.2), kind=kOutput, calls=%fused_computation.1.clone.1 | convolution fusion | flops 67371008 | bytes 2621476 | tf_op jit(solution)/shard_map/while/body/pkc,kcn->pkn/dot_general | solution.py:25
  137.7 21.3 %reduce-scatter.2.cloned.1.call-done = f32[16,2048]{1,0:T(8,128)} async-done(((f32[64,2048]{1,0:T(8,128)}), f32[16,2048]{1,0:T(8,128)}) %reduce-scatter.2.cloned.1.call-update) | async-done | bytes 131088 | tf_op jit(solution)/shard_map/reduce_scatter | solution.py:48
  158.9 1.5 convert_element_type.11
  (55 shorter events, 16.0 us)
Async XLA Ops:
  6.5 74.4 %all-gather.2.cloned.1.call-start = ((), (), s32[]{:S(2)}) async-start(), calls=%async_computation.2 | async-start | bytes 3686400 | tf_op jit(solution)/shard_map/all_gather | solution.py:42
  18.9 140.0 %reduce-scatter.2.cloned.1.call-start = ((), (), s32[]{:S(2)}) async-start(), calls=%async_computation.3 | async-start | bytes 655360 | tf_op jit(solution)/shard_map/reduce_scatter | solution.py:48
  19.6 65.8 %copy-start = (s32[256,2]{0,1:T(2,128)S(1)}, s32[256,2]{0,1:T(2,128)}, u32[]{:S(2)}) copy-start(s32[256,2]{0,1:T(2,128)} %param.8) | copy-start | bytes 6148
Sparse Core Ops, SparseCore 0:
  19.0 61.8 all-gather.1
  137.8 21.1 reduce-scatter.1
where the time goes:
time: 169 us; the launch traced here: 167 us
  waiting for transfers between devices  82.6 us (49%)
  local copies, waits for them, and re-layouts  27.6 us (16%)
  matrix products  24.1 us (14%)
  between operations  14.1 us (8%)
  blocking collectives  11.4 us (7%)
  other arithmetic  6.98 us (4%)
    all_gather x1, waiting for transfers between devices, per_device(): lax.all_gather(columns, 'vp', axis=0, tiled=True)  61.3 us
    reduce_scatter x1, waiting for transfers between devices, per_device(): lax.psum_scatter(partial_value, 'vc', scatter_dimension=0, tiled=True)  21.3 us
    gather x8, local copies, waits for them, and re-layouts, add_block(): picked = jnp.take(grouped, indices[:, 1], axis=1)  20.6 us
    dot_general x8, matrix products, add_block(): jnp.einsum('pkc,kcn->pkn', picked, tiles_block, preferred_element_type=jn...  13.5 us
    all_to_all x1, blocking collectives, per_device(): lax.all_to_all(amplitudes, 'vc', split_axis=1, concat_axis=0, tiled=True)  11.4 us
    dot_general x8, matrix products, add_block(): jnp.einsum('pkn,ka->pan', product, select, precision=lax.Precision.HIGHEST)  10.7 us
    convert_element_type x8, other arithmetic, add_block(): alive_mask = (slot_ids < end_slot).astype(jnp.float32)  5.23 us
    while x1, local copies, waits for them, and re-layouts, accumulate(): totals = lax.fori_loop(0, end_block, add_block, start_totals)  4.54 us
  transfers between devices with their start and end apart: 2, of which 2 were waited for; matrix products, arithmetic and copies ran while one was open for 0% of the time, Pallas kernels for 0%

commit v1 on v0

v1 whole, which is shorter than its diff:
```python
import functools

import jax
import jax.numpy as jnp
from jax import lax
from jax.experimental import pallas as pl
from jax.experimental.pallas import tpu as pltpu
from jax.sharding import PartitionSpec as P

AB_TILES = 16
SLOW = 4
VMEM = 56 * 1024 * 1024
MESH = pl.DeviceIdType.MESH


def largest_divisor(value, limit):
    return max(d for d in range(1, limit + 1) if value % d == 0)


def gather_kernel(dims, amp_ref, full_ref, pieces, piece_send, piece_recv,
                  up_send, down_send, chain_recv, side_send, side_recv):
    slow, fast, vcs, tiles, chunks = dims
    share = tiles // fast
    size = share // chunks
    group = fast * vcs
    vp = lax.axis_index("vp")
    c = lax.axis_index("vc")
    a, b = lax.div(vp, fast), lax.rem(vp, fast)
    me = b * vcs + c

    def in_plane(step):
        other = lax.rem(me + step, group)
        return lax.div(other, vcs), lax.rem(other, vcs)

    def plane_id(ob, oc):
        return (a * fast + ob, oc)

    barrier = pltpu.get_barrier_semaphore()

    def greet(step, carry):
        ob, oc = in_plane(step)
        pl.semaphore_signal(barrier, inc=1, device_id=plane_id(ob, oc), device_id_type=MESH)
        return carry

    lax.fori_loop(1, group, greet, 0)

    @pl.when(a > 0)
    def _():
        pl.semaphore_signal(barrier, inc=1, device_id=(vp - fast, c), device_id_type=MESH)

    @pl.when(a < slow - 1)
    def _():
        pl.semaphore_signal(barrier, inc=1, device_id=(vp + fast, c), device_id_type=MESH)

    edges = (a > 0).astype(jnp.int32) + (a < slow - 1).astype(jnp.int32)
    pl.semaphore_wait(barrier, group - 1 + edges)

    def piece_copy(k, step):
        ob, oc = in_plane(step)
        return pltpu.make_async_remote_copy(
            src_ref=amp_ref.at[pl.ds(oc * tiles + ob * share + k * size, size)],
            dst_ref=pieces.at[me, pl.ds(k * size, size)],
            send_sem=piece_send, recv_sem=piece_recv.at[k],
            device_id=plane_id(ob, oc), device_id_type=MESH)

    def send_pieces(k, carry):
        def one(step, carry):
            piece_copy(k, step).start()
            return carry
        return lax.fori_loop(1, group, one, carry)

    lax.fori_loop(0, chunks, send_pieces, 0)
    pieces[me] = amp_ref[pl.ds(c * tiles + b * share, share)]

    def block(plane, k):
        return full_ref.at[plane, pl.ds(b * share + k * size, size)]

    def up(plane, k):
        return pltpu.make_async_remote_copy(
            src_ref=block(plane, k), dst_ref=block(plane, k),
            send_sem=up_send.at[plane, k], recv_sem=chain_recv.at[plane, k],
            device_id=(vp + fast, c), device_id_type=MESH)

    def down(plane, k):
        return pltpu.make_async_remote_copy(
            src_ref=block(plane, k), dst_ref=block(plane, k),
            send_sem=down_send.at[plane, k], recv_sem=chain_recv.at[plane, k],
            device_id=(vp - fast, c), device_id_type=MESH)

    def sideways(plane, k):
        def one(step, carry):
            ob = lax.rem(b + step, fast)
            pltpu.make_async_remote_copy(
                src_ref=block(plane, k), dst_ref=block(plane, k),
                send_sem=side_send, recv_sem=side_recv,
                device_id=plane_id(ob, c), device_id_type=MESH).start()
            return carry
        lax.fori_loop(1, fast, one, 0)

    def own_chunk(k, carry):
        arrived = pieces.at[pl.ds(0, group - 1), pl.ds(k * size, size)]
        pltpu.make_async_copy(arrived, arrived, piece_recv.at[k]).wait()
        full_ref[a, pl.ds(b * share + k * size, size)] = jnp.concatenate(
            [pieces[i, pl.ds(k * size, size)] for i in range(group)], axis=1)

        @pl.when(a > 0)
        def _():
            down(a, k).start()

        @pl.when(a < slow - 1)
        def _():
            up(a, k).start()

        sideways(a, k)
        return carry

    lax.fori_loop(0, chunks, own_chunk, 0)

    for far in range(1, slow):
        def passed_chunk(k, carry, far=far):
            @pl.when(a - far >= 0)
            def _():
                up(a - far, k).wait_recv()

                @pl.when(a < slow - 1)
                def _():
                    up(a - far, k).start()

                sideways(a - far, k)

            @pl.when(a + far < slow)
            def _():
                down(a + far, k).wait_recv()

                @pl.when(a > 0)
                def _():
                    down(a + far, k).start()

                sideways(a + far, k)

            return carry

        lax.fori_loop(0, chunks, passed_chunk, 0)

    if fast > 1:
        moved = full_ref.at[:, pl.ds(0, (fast - 1) * share)]
        pltpu.make_async_copy(moved, moved, side_recv).wait()
        pltpu.make_async_copy(moved, moved, side_send).wait()
    sent = pieces.at[pl.ds(0, group - 1)]
    pltpu.make_async_copy(sent, sent, piece_send).wait()

    for far in range(slow):
        def sent_chunk(k, carry, far=far):
            @pl.when((a - far >= 0) & (a < slow - 1))
            def _():
                up(a - far, k).wait_send()

            @pl.when((a + far < slow) & (a > 0))
            def _():
                down(a + far, k).wait_send()

            return carry

        lax.fori_loop(0, chunks, sent_chunk, 0)


def ladder_kernel(batch, parts, pairs_ref, count_ref, full_ref, tiles_hbm, out_ref, tiles, sems):
    slots = tiles.shape[0]
    part = slots // parts
    width = tiles.shape[1]
    rows = full_ref.shape[0] * full_ref.shape[2]
    out_parts, _, out_rows, _ = out_ref.shape

    def fetch(i):
        window = pl.ds(i * part, part)
        return pltpu.make_async_copy(tiles_hbm.at[window], tiles.at[window], sems.at[i])

    for i in range(parts):
        fetch(i).start()
    out_ref[...] = jnp.zeros_like(out_ref)
    count = count_ref[0]
    for i in range(parts):
        fetch(i).wait()

        def step(j, carry, i=i):
            base = i * part + j * batch

            @pl.when(base < count)
            def _():
                products = []
                for n in range(batch):
                    left = full_ref[:, pairs_ref[2 * (base + n) + 1]].reshape(rows, width)
                    products.append(jnp.dot(left, tiles[base + n], preferred_element_type=jnp.float32))
                for n in range(batch):
                    ab = pairs_ref[2 * (base + n)]
                    live = base + n < count
                    term = jnp.where(live, products[n], 0.0).reshape(out_parts, out_rows, width)
                    out_ref[:, ab] += term

            return carry

        lax.fori_loop(0, part // batch, step, 0)


def sum_kernel(parts, part_ref, out_ref, arrived, send_sem, recv_sem):
    c = lax.axis_index("vc")
    vp = lax.axis_index("vp")
    barrier = pltpu.get_barrier_semaphore()
    for step in range(1, parts):
        pl.semaphore_signal(barrier, inc=1, device_id=(vp, lax.rem(c + step, parts)), device_id_type=MESH)
    pl.semaphore_wait(barrier, parts - 1)
    copies = []
    for step in range(1, parts):
        other = lax.rem(c + step, parts)
        copy = pltpu.make_async_remote_copy(
            src_ref=part_ref.at[other], dst_ref=arrived.at[step - 1],
            send_sem=send_sem.at[step - 1], recv_sem=recv_sem.at[step - 1],
            device_id=(vp, other), device_id_type=MESH)
        copy.start()
        copies.append(copy)
    for copy in copies:
        copy.wait_recv()
    width = part_ref.shape[3]
    for i in range(part_ref.shape[1]):
        total = part_ref[c, i]
        for step in range(parts - 1):
            total += arrived[step, i]
        out_ref[:, i * width:(i + 1) * width] = total.astype(out_ref.dtype)
    for copy in copies:
        copy.wait_send()


def per_device(n_vp, n_vc, amplitudes, pair_tiles, slot_pairs, slot_count):
    own_rows, columns = amplitudes.shape
    slots, width, _ = pair_tiles.shape
    slow = SLOW if n_vp % SLOW == 0 else n_vp
    fast = n_vp // slow
    tiles = columns // width // n_vc
    rows = own_rows * n_vp * n_vc
    plane_rows = rows // slow
    share = tiles // fast
    chunks = largest_divisor(share, 5)
    group = fast * n_vc
    in_vmem = pl.BlockSpec(memory_space=pltpu.VMEM)

    amp = amplitudes.reshape(own_rows, columns // width, width).transpose(1, 0, 2)
    full = pl.pallas_call(
        functools.partial(gather_kernel, (slow, fast, n_vc, tiles, chunks)),
        out_shape=jax.ShapeDtypeStruct((slow, tiles, plane_rows, width), amplitudes.dtype),
        in_specs=[in_vmem],
        out_specs=in_vmem,
        scratch_shapes=[
            pltpu.VMEM((group, share, own_rows, width), amplitudes.dtype),
            pltpu.SemaphoreType.DMA,
            pltpu.SemaphoreType.DMA((chunks,)),
            pltpu.SemaphoreType.DMA((slow, chunks)),
            pltpu.SemaphoreType.DMA((slow, chunks)),
            pltpu.SemaphoreType.DMA((slow, chunks)),
            pltpu.SemaphoreType.DMA,
            pltpu.SemaphoreType.DMA,
        ],
        compiler_params=pltpu.CompilerParams(
            collective_id=0, has_side_effects=True, vmem_limit_bytes=VMEM),
        name="gather_amplitudes",
    )(amp)

    out_rows = rows // n_vc
    parts = largest_divisor(slots, 8)
    batch = largest_divisor(slots // parts, max(1, 1024 // rows))
    in_smem = pl.BlockSpec(memory_space=pltpu.SMEM)
    partial = pl.pallas_call(
        functools.partial(ladder_kernel, batch, parts),
        out_shape=jax.ShapeDtypeStruct((n_vc, AB_TILES, out_rows, width), jnp.float32),
        in_specs=[in_smem, in_smem, in_vmem, pl.BlockSpec(memory_space=pl.ANY)],
        out_specs=in_vmem,
        scratch_shapes=[
            pltpu.VMEM(pair_tiles.shape, pair_tiles.dtype),
            pltpu.SemaphoreType.DMA((parts,)),
        ],
        compiler_params=pltpu.CompilerParams(vmem_limit_bytes=VMEM),
        name="ladder",
    )(slot_pairs.reshape(-1), slot_count, full, pair_tiles)

    return pl.pallas_call(
        functools.partial(sum_kernel, n_vc),
        out_shape=jax.ShapeDtypeStruct((out_rows, AB_TILES * width), jnp.bfloat16),
        in_specs=[in_vmem],
        out_specs=in_vmem,
        scratch_shapes=[
            pltpu.VMEM((n_vc - 1, AB_TILES, out_rows, width), jnp.float32),
            pltpu.SemaphoreType.DMA((n_vc - 1,)),
            pltpu.SemaphoreType.DMA((n_vc - 1,)),
        ],
        compiler_params=pltpu.CompilerParams(
            collective_id=1, has_side_effects=True, vmem_limit_bytes=VMEM),
        name="sum_partials",
    )(partial)


def solution(mesh):
    in_specs = (
        P(("vp", "vc"), None),
        P(("vp", "vc"), None, None),
        P(("vp", "vc"), None),
        P(("vp", "vc")),
    )
    return jax.shard_map(
        functools.partial(per_device, mesh.shape["vp"], mesh.shape["vc"]),
        mesh=mesh, in_specs=in_specs, out_specs=P("vc", "vp"), check_vma=False)
```

time: 169 us -> 70.4 us (0.42)
  waiting for transfers between devices: 82.6 us -> 0 us
  Pallas kernels: 0 us -> 66.6 us
  local copies, waits for them, and re-layouts: 27.6 us -> 3.01 us
  matrix products: 24.1 us -> 0 us
  between operations: 14.1 us -> 0.68 us
  blocking collectives: 11.4 us -> 0 us
  other arithmetic: 6.98 us -> 0 us
    pallas_call x0 -> x3, Pallas kernels: none -> 66.6 us  [the longest x1 47.8 us: per_device(): pl.pallas_call(functools.partial(gather_kernel, (slow, fast, n_vc, tiles,...]
    all_gather x1 -> x0, waiting for transfers between devices: 61.3 us -> none  [per_device(): lax.all_gather(columns, 'vp', axis=0, tiled=True)]
    dot_general x16 -> x0, matrix products: 24.1 us -> none  [the longest x8 13.5 us: add_block(): jnp.einsum('pkc,kcn->pkn', picked, tiles_block, preferred_element_type=jn...]
    reduce_scatter x1 -> x0, waiting for transfers between devices: 21.3 us -> none  [per_device(): lax.psum_scatter(partial_value, 'vc', scatter_dimension=0, tiled=True)]
    gather x8 -> x0, local copies, waits for them, and re-layouts: 20.6 us -> none  [add_block(): picked = jnp.take(grouped, indices[:, 1], axis=1)]
    all_to_all x1 -> x0, blocking collectives: 11.4 us -> none  [per_device(): lax.all_to_all(amplitudes, 'vc', split_axis=1, concat_axis=0, tiled=True)]
    convert_element_type x9 -> x0, other arithmetic: 6.77 us -> none  [the longest x8 5.23 us: add_block(): alive_mask = (slot_ids < end_slot).astype(jnp.float32)]
    while x1 -> x0, local copies, waits for them, and re-layouts: 4.54 us -> none  [accumulate(): totals = lax.fori_loop(0, end_block, add_block, start_totals)]
  transfers between devices with their start and end apart: 2 -> 0, of which waited for: 2 -> 0; matrix products, arithmetic and copies ran while one was open for 0% -> 0% of each run, Pallas kernels for 0% -> 0%
where the time goes in v1:
time: 70.4 us; the launch traced here: 70.3 us
  Pallas kernels  66.6 us (95%)
  local copies, waits for them, and re-layouts  3.01 us (4%)
    pallas_call x1, Pallas kernels, per_device(): pl.pallas_call(functools.partial(gather_kernel, (slow, fast, n_vc, tiles,...  47.8 us
    pallas_call x1, Pallas kernels, per_device(): pl.pallas_call(functools.partial(sum_kernel, n_vc), out_shape=jax.ShapeDt...  10.2 us
    pallas_call x1, Pallas kernels, per_device(): pl.pallas_call(functools.partial(ladder_kernel, batch, parts), out_shape=...  8.55 us
    unnamed x2, local copies, waits for them, and re-layouts  2.28 us

profile of v1, /device:TPU:1, one launch (start us, length us, event | category | flops | bytes accessed | tf_op | source)
XLA Modules:
  0.0 70.3 jit_solution(13216503324483716574)
XLA Ops:
  0.7 0.8 %copy.5 = s32[256,2]{1,0:T(8,128)S(1)} copy(s32[256,2]{0,1:T(2,128)} %param.6) | data formatting | bytes 4096 | tf_op args[2]
  1.5 0.7 %reshape.6.pairs_ref = s32[512]{0:T(512)} reshape(s32[256,2]{1,0:T(8,128)S(1)} %copy.5) | data formatting | bytes 4096 | tf_op jit(solution)/shard_map/reshape | solution.py:282
  2.2 47.8 %gather_amplitudes.1.full_ref = bf16[4,200,16,128]{3,2,1,0:T(8,128)(2,1)} custom-call(bf16[800,2,128]{2,1,0:T(2,128)(2,1)} %bitcast.3), custom_call_target="tpu_custom_call" | custom-call | tf_op jit(solution)/shard_map/gather_amplitudes/pallas_call | solution.py:247
  50.0 8.5 %ladder.1.part_ref = f32[4,16,16,128]{3,2,1,0:T(8,128)} custom-call(s32[512]{0:T(512)} %reshape.6.pairs_ref, s32[1]{0:T(128)S(6)} %copy.7.count_ref, bf16[4,200,16,128]{3,2,1,0:T(8,128)(2,1)} %gather_amplitudes.1.full_ref, bf16[256,128,128]{2,1,0:T(8,128)(2,1)} %tiles_hbm.1), custom_call_target="tpu_custom_call" | custom-call | tf_op jit(solution)/shard_map/ladder/pallas_call | solution.py:271
  58.6 10.2 %sum_partials.1 = bf16[16,2048]{1,0:T(8,128)(2,1)} custom-call(f32[4,16,16,128]{3,2,1,0:T(8,128)} %ladder.1.part_ref), custom_call_target="tpu_custom_call" | custom-call | tf_op jit(solution)/shard_map/sum_partials/pallas_call | solution.py:284
  68.8 1.5 %copy.8 = bf16[16,2048]{1,0:T(8,128)(2,1)} copy(bf16[16,2048]{1,0:T(8,128)(2,1)} %sum_partials.1) | data formatting | bytes 131072
